TPU v7x, 512 devices: a whole 4x4x16 slice. The times are simulated.
512 devices in a mesh: ctx: 64 (over y, z), head: 8 (over x, core).
Axes of the slice: x: 4, y: 4, z: 16, core: 2. Of those that a mesh axis runs over, the one named last changes fastest.
Arguments:
- queries: bfloat16 [8192, 64, 576], P('ctx', 'head'), may hold values from -14 to 14
- latents: bfloat16 [8192, 576], P('ctx'), may hold values from -6 to 6
- grad_out: bfloat16 [8192, 64, 512], P('ctx', 'head'), may hold values from -6 to 6
- doc_ids: int32 [8192], replicated, may hold values from 0 to 8191, as said below
Outputs:
- grad_queries: bfloat16 [8192, 64, 576], P('ctx', 'head')
- grad_latents: bfloat16 [8192, 576], P('ctx')
Inputs may be any that keep to these rules, and one draw needn't show every extreme that they name: `doc_ids`: each document is a contiguous run of at most 1024 tokens, one has exactly that many, and its label is the position of its first token.
All inputs are finite; a program needn't handle non-finite values.
Results may differ from a plain program's by a relative error of at most 0.0052.
Values may be sent and summed in bfloat16 or wider, within the bound.
A program may use at most 64 MiB of HBM per device.

v0:
```python
import jax
import jax.numpy as jnp
from jax import lax
from jax.sharding import PartitionSpec as P

LAT_C = 512
ROPE = 64
SPAN = 8
score_scale = 192.0 ** (-0.5)


def passed_along(value, axis, steps):
    count = lax.axis_size(axis)
    leading, last = (max(0, -steps), min(count, count - steps))
    return lax.ppermute(value, axis, [(source, source + steps) for source in range(leading, last)])


def attend_backward(query_rows, grad_rows, key_rows, visible):
    value_rows = key_rows[:, :LAT_C]
    scores = (
        jnp.einsum("thc,kc->htk", query_rows, key_rows, preferred_element_type=jnp.float32)
        * score_scale
    )
    scores = jnp.where(visible[None], scores, -1e30)
    row_max = jnp.max(scores, axis=-1, keepdims=True)
    expo = jnp.where(visible[None], jnp.exp(scores - row_max), 0.0)
    weights = expo / jnp.sum(expo, axis=-1, keepdims=True)
    probs = weights.astype(jnp.bfloat16)
    output = jnp.einsum("htk,kc->thc", probs, value_rows, preferred_element_type=jnp.float32)
    delta = jnp.sum(grad_rows.astype(jnp.float32) * output, axis=-1)
    grad_probs = jnp.einsum(
        "thc,kc->htk", grad_rows, value_rows, preferred_element_type=jnp.float32
    )
    grad_scores = (weights * (grad_probs - jnp.transpose(delta)[:, :, None]) * score_scale).astype(
        jnp.bfloat16
    )
    grad_query = jnp.einsum(
        "htk,kc->thc", grad_scores, key_rows, preferred_element_type=jnp.float32
    ).astype(jnp.bfloat16)
    grad_keys = jnp.einsum(
        "htk,thc->kc", grad_scores, query_rows, preferred_element_type=jnp.float32
    )
    grad_values = jnp.einsum("htk,thc->kc", probs, grad_rows, preferred_element_type=jnp.float32)
    grad_keys = grad_keys + jnp.pad(grad_values, ((0, 0), (0, ROPE)))
    return (grad_query, grad_keys)


def return_owned(window_grads, tok_rows):
    owned = window_grads[SPAN * tok_rows :]
    for offset in range(1, SPAN + 1):
        piece = window_grads[(SPAN - offset) * tok_rows : (SPAN - offset + 1) * tok_rows]
        owned = owned + passed_along(piece, "ctx", -offset)
    return owned


def on_device(queries, latents, grad_out, doc_ids):
    tok_rows = latents.shape[0]
    window = (SPAN + 1) * tok_rows
    shard_index = lax.axis_index("ctx")
    pieces = []
    for offset in range(SPAN, 0, -1):
        pieces.append(passed_along(latents, "ctx", offset))
    pieces.append(latents)
    key_rows = jnp.concatenate(pieces, axis=0)
    start = shard_index * tok_rows
    padded_ids = jnp.concatenate([jnp.full((SPAN * tok_rows,), -1, jnp.int32), doc_ids], axis=0)
    key_ids = lax.dynamic_slice_in_dim(padded_ids, start, window, 0)
    query_ids = lax.dynamic_slice_in_dim(doc_ids, start, tok_rows, 0)
    query_pos = start + jnp.arange(tok_rows, dtype=jnp.int32)
    key_pos = start - SPAN * tok_rows + jnp.arange(window, dtype=jnp.int32)
    visible = (key_ids[None, :] == query_ids[:, None]) & (key_pos[None, :] <= query_pos[:, None])
    grad_query, grad_keys = attend_backward(queries, grad_out, key_rows, visible)
    owned = lax.psum(return_owned(grad_keys, tok_rows), "head")
    return (grad_query, owned.astype(jnp.bfloat16))


def solution(mesh):
    placed = (P("ctx", "head", None), P("ctx", None), P("ctx", "head", None), P())
    return jax.shard_map(
        on_device,
        mesh=mesh,
        in_specs=placed,
        out_specs=(P("ctx", "head", None), P("ctx", None)),
        check_vma=False,
    )
```

profile of v0, /device:TPU:16, one launch (start us, length us, event | category | flops | bytes accessed | tf_op | source)
XLA Modules:
  0.0 377.0 jit_solution(13197455609883375270)
XLA Ops:
  0.7 15.9 %collective-permute-start = (bf16[128,576]{0,1:T(8,128)(2,1)}, bf16[128,576]{0,1:T(8,128)(2,1)S(1)}, u32[]{:S(2)}, u32[]{:S(2)}) collective-permute-start(bf16[128,576]{0,1:T(8,128)(2,1)} %param.5), channel_id=1, source_target_pairs={{0,64},{8,72},{16,80},{24,88},{32,96},{40,104},{48,112},{56,120},{... | collective-permute-start | bytes 442376 | tf_op jit(solution)/shard_map/ppermute | solution.py:15
  16.5 5.7 %collective-permute-start.1 = (bf16[128,576]{0,1:T(8,128)(2,1)}, bf16[128,576]{0,1:T(8,128)(2,1)S(1)}, u32[]{:S(2)}, u32[]{:S(2)}) collective-permute-start(bf16[128,576]{0,1:T(8,128)(2,1)} %param.5), channel_id=1, source_target_pairs={{0,56},{8,64},{16,72},{24,80},{32,88},{40,96},{48,104},{56,112},{6... | collective-permute-start | bytes 442376 | tf_op jit(solution)/shard_map/ppermute | solution.py:15
  26.5 8.7 %collective-permute-start.3 = (bf16[128,576]{0,1:T(8,128)(2,1)}, bf16[128,576]{0,1:T(8,128)(2,1)S(1)}, u32[]{:S(2)}, u32[]{:S(2)}) collective-permute-start(bf16[128,576]{0,1:T(8,128)(2,1)} %param.5), channel_id=1, source_target_pairs={{0,40},{8,48},{16,56},{24,64},{32,72},{40,80},{48,88},{56,96},{64,... | collective-permute-start | bytes 442376 | tf_op jit(solution)/shard_map/ppermute | solution.py:15
  46.4 18.1 %collective-permute-done.1 = bf16[128,576]{0,1:T(8,128)(2,1)S(1)} collective-permute-done((bf16[128,576]{0,1:T(8,128)(2,1)}, bf16[128,576]{0,1:T(8,128)(2,1)S(1)}, u32[]{:S(2)}, u32[]{:S(2)}) %collective-permute-start.1) | collective-permute-done | bytes 147488 | tf_op jit(solution)/shard_map/ppermute | solution.py:15
  64.6 8.2 %collective-permute-start.6 = (bf16[128,576]{0,1:T(8,128)(2,1)S(1)}, bf16[128,576]{0,1:T(8,128)(2,1)S(1)}, u32[]{:S(2)}, u32[]{:S(2)}) collective-permute-start(bf16[128,576]{0,1:T(8,128)(2,1)S(1)} %copy-done.1), channel_id=1, source_target_pairs={{0,16},{8,24},{16,32},{24,40},{32,48},{40,56},{48,64},{56,72},{64,... | collective-permute-start | bytes 442376 | tf_op jit(solution)/shard_map/ppermute | solution.py:15
  73.5 5.4 %collective-permute-start.7 = (bf16[128,576]{0,1:T(8,128)(2,1)S(1)}, bf16[128,576]{0,1:T(8,128)(2,1)S(1)}, u32[]{:S(2)}, u32[]{:S(2)}) collective-permute-start(bf16[128,576]{0,1:T(8,128)(2,1)S(1)} %copy-done.1), channel_id=1, source_target_pairs={{0,8},{8,16},{16,24},{24,32},{32,40},{40,48},{48,56},{56,64},{64,7... | collective-permute-start | bytes 442376 | tf_op jit(solution)/shard_map/ppermute | solution.py:15
  79.6 11.8 %collective-permute-done.3 = bf16[128,576]{0,1:T(8,128)(2,1)S(1)} collective-permute-done((bf16[128,576]{0,1:T(8,128)(2,1)}, bf16[128,576]{0,1:T(8,128)(2,1)S(1)}, u32[]{:S(2)}, u32[]{:S(2)}) %collective-permute-start.3) | collective-permute-done | bytes 147488 | tf_op jit(solution)/shard_map/ppermute | solution.py:15
  92.7 15.1 %collective-permute-done.5 = bf16[128,576]{0,1:T(8,128)(2,1)S(1)} collective-permute-done((bf16[128,576]{0,1:T(8,128)(2,1)S(1)}, bf16[128,576]{0,1:T(8,128)(2,1)S(1)}, u32[]{:S(2)}, u32[]{:S(2)}) %collective-permute-start.5) | collective-permute-done | bytes 147488 | tf_op jit(solution)/shard_map/ppermute | solution.py:15
  108.5 6.1 %collective-permute-done.6 = bf16[128,576]{0,1:T(8,128)(2,1)S(1)} collective-permute-done((bf16[128,576]{0,1:T(8,128)(2,1)S(1)}, bf16[128,576]{0,1:T(8,128)(2,1)S(1)}, u32[]{:S(2)}, u32[]{:S(2)}) %collective-permute-start.6) | collective-permute-done | bytes 147488 | tf_op jit(solution)/shard_map/ppermute | solution.py:15
  119.1 6.8 %fusion.25 = (f32[8,128]{1,0:T(8,128)S(1)}, f32[8,128,1152]{1,2,0:T(8,128)}) fusion(pred[128,1152]{0,1:T(8,128)(4,1)S(1)} %compare_and_fusion, bf16[128,8,576]{0,2,1:T(8,128)(2,1)S(1)} %copy-done, bf16[1152,576]{0,1:T(8,128)(2,1)} %constant_dynamic-update-slice_fusion), kind=kOutput, calls=%fused_computation.47 | convolution fusion | flops 1364853888 | bytes 7376896 | tf_op jit(solution)/shard_map/sub | solution.py:26
  136.9 9.2 %collective-permute-start.15 = (f32[128,576]{0,1:T(8,128)S(1)}, f32[128,576]{0,1:T(8,128)S(1)}, u32[]{:S(2)}, u32[]{:S(2)}) collective-permute-start(f32[128,576]{0,1:T(8,128)S(1)} %get-tuple-element.3), channel_id=1, source_target_pairs={{64,0},{72,8},{80,16},{88,24},{96,32},{104,40},{112,48},{120,56},{... | collective-permute-start | bytes 884744 | tf_op jit(solution)/shard_map/ppermute | solution.py:15
  146.1 5.5 %collective-permute-start.14 = (f32[128,576]{0,1:T(8,128)S(1)}, f32[128,576]{0,1:T(8,128)S(1)}, u32[]{:S(2)}, u32[]{:S(2)}) collective-permute-start(f32[128,576]{0,1:T(8,128)S(1)} %get-tuple-element.4), channel_id=1, source_target_pairs={{56,0},{64,8},{72,16},{80,24},{88,32},{96,40},{104,48},{112,56},{1... | collective-permute-start | bytes 884744 | tf_op jit(solution)/shard_map/ppermute | solution.py:15
  155.7 8.4 %collective-permute-start.12 = (f32[128,576]{0,1:T(8,128)S(1)}, f32[128,576]{0,1:T(8,128)S(1)}, u32[]{:S(2)}, u32[]{:S(2)}) collective-permute-start(f32[128,576]{0,1:T(8,128)S(1)} %get-tuple-element.6), channel_id=1, source_target_pairs={{40,0},{48,8},{56,16},{64,24},{72,32},{80,40},{88,48},{96,56},{104... | collective-permute-start | bytes 884744 | tf_op jit(solution)/shard_map/ppermute | solution.py:15
  164.1 4.5 %collective-permute-start.11 = (f32[128,576]{0,1:T(8,128)S(1)}, f32[128,576]{0,1:T(8,128)S(1)}, u32[]{:S(2)}, u32[]{:S(2)}) collective-permute-start(f32[128,576]{0,1:T(8,128)S(1)} %get-tuple-element.7), channel_id=1, source_target_pairs={{32,0},{40,8},{48,16},{56,24},{64,32},{72,40},{80,48},{88,56},{96,... | collective-permute-start | bytes 884744 | tf_op jit(solution)/shard_map/ppermute | solution.py:15
  168.5 7.0 %collective-permute-done.15 = f32[128,576]{0,1:T(8,128)S(1)} collective-permute-done((f32[128,576]{0,1:T(8,128)S(1)}, f32[128,576]{0,1:T(8,128)S(1)}, u32[]{:S(2)}, u32[]{:S(2)}) %collective-permute-start.15) | collective-permute-done | bytes 294944 | tf_op jit(solution)/shard_map/ppermute | solution.py:15
  177.5 29.1 %collective-permute-done.14 = f32[128,576]{0,1:T(8,128)S(1)} collective-permute-done((f32[128,576]{0,1:T(8,128)S(1)}, f32[128,576]{0,1:T(8,128)S(1)}, u32[]{:S(2)}, u32[]{:S(2)}) %collective-permute-start.14) | collective-permute-done | bytes 294944 | tf_op jit(solution)/shard_map/ppermute | solution.py:15
  206.6 22.0 %collective-permute-start.9 = (f32[128,576]{0,1:T(8,128)S(1)}, f32[128,576]{0,1:T(8,128)S(1)}, u32[]{:S(2)}, u32[]{:S(2)}) collective-permute-start(f32[128,576]{0,1:T(8,128)S(1)} %get-tuple-element.9), channel_id=1, source_target_pairs={{16,0},{24,8},{32,16},{40,24},{48,32},{56,40},{64,48},{72,56},{80,... | collective-permute-start | bytes 884744 | tf_op jit(solution)/shard_map/ppermute | solution.py:15
  228.7 26.3 %collective-permute-done.13 = f32[128,576]{0,1:T(8,128)S(1)} collective-permute-done((f32[128,576]{0,1:T(8,128)S(1)}, f32[128,576]{0,1:T(8,128)S(1)}, u32[]{:S(2)}, u32[]{:S(2)}) %collective-permute-start.13) | collective-permute-done | bytes 294944 | tf_op jit(solution)/shard_map/ppermute | solution.py:15
  260.9 24.9 %collective-permute-done.12 = f32[128,576]{0,1:T(8,128)S(1)} collective-permute-done((f32[128,576]{0,1:T(8,128)S(1)}, f32[128,576]{0,1:T(8,128)S(1)}, u32[]{:S(2)}, u32[]{:S(2)}) %collective-permute-start.12) | collective-permute-done | bytes 294944 | tf_op jit(solution)/shard_map/ppermute | solution.py:15
  285.8 25.1 %collective-permute-done.11 = f32[128,576]{0,1:T(8,128)S(1)} collective-permute-done((f32[128,576]{0,1:T(8,128)S(1)}, f32[128,576]{0,1:T(8,128)S(1)}, u32[]{:S(2)}, u32[]{:S(2)}) %collective-permute-start.11) | collective-permute-done | bytes 294944 | tf_op jit(solution)/shard_map/ppermute | solution.py:15
  311.0 17.8 %collective-permute-done.10 = f32[128,576]{0,1:T(8,128)S(1)} collective-permute-done((f32[128,576]{0,1:T(8,128)S(1)}, f32[128,576]{0,1:T(8,128)S(1)}, u32[]{:S(2)}, u32[]{:S(2)}) %collective-permute-start.10) | collective-permute-done | bytes 294944 | tf_op jit(solution)/shard_map/ppermute | solution.py:15
  328.7 12.5 %collective-permute-done.9 = f32[128,576]{0,1:T(8,128)S(1)} collective-permute-done((f32[128,576]{0,1:T(8,128)S(1)}, f32[128,576]{0,1:T(8,128)S(1)}, u32[]{:S(2)}, u32[]{:S(2)}) %collective-permute-start.9) | collective-permute-done | bytes 294944 | tf_op jit(solution)/shard_map/ppermute | solution.py:15
  341.2 6.3 %collective-permute-done.8 = f32[128,576]{0,1:T(8,128)S(1)} collective-permute-done((f32[128,576]{0,1:T(8,128)S(1)}, f32[128,576]{0,1:T(8,128)S(1)}, u32[]{:S(2)}, u32[]{:S(2)}) %collective-permute-start.8) | collective-permute-done | bytes 294944 | tf_op jit(solution)/shard_map/ppermute | solution.py:15
  347.7 29.4 %all-reduce.3 = bf16[128,576]{0,1:T(8,128)(2,1)} all-reduce(f32[128,576]{0,1:T(8,128)S(1)} %fusion.20), channel_id=1, replica_groups=mesh['ctx'=64,'head'=8] {'head'}, use_global_device_ids=true, to_apply=%region_3.4 | all-reduce | flops 73728 | bytes 442368 | tf_op jit(solution)/shard_map/psum | solution.py:73
  (37 shorter events, 46.4 us)
Async XLA Ops:
  0.6 118.4 %copy-start = (bf16[128,8,576]{0,2,1:T(8,128)(2,1)S(1)}, bf16[128,8,576]{0,2,1:T(8,128)(2,1)}, u32[]{:S(2)}) copy-start(bf16[128,8,576]{0,2,1:T(8,128)(2,1)} %param.4) | copy-start | bytes 3538948
  0.6 43.2 %copy-start.1 = (bf16[128,576]{0,1:T(8,128)(2,1)S(1)}, bf16[128,576]{0,1:T(8,128)(2,1)}, u32[]{:S(2)}) copy-start(bf16[128,576]{0,1:T(8,128)(2,1)} %param.5) | copy-start | bytes 442372
  0.7 43.1 %collective-permute-start = (bf16[128,576]{0,1:T(8,128)(2,1)}, bf16[128,576]{0,1:T(8,128)(2,1)S(1)}, u32[]{:S(2)}, u32[]{:S(2)}) collective-permute-start(bf16[128,576]{0,1:T(8,128)(2,1)} %param.5), channel_id=1, source_target_pairs={{0,64},{8,72},{16,80},{24,88},{32,96},{40,104},{48,112},{56,120},{... | collective-permute-start | bytes 442376 | tf_op jit(solution)/shard_map/ppermute | solution.py:15
  16.5 48.1 %collective-permute-start.1 = (bf16[128,576]{0,1:T(8,128)(2,1)}, bf16[128,576]{0,1:T(8,128)(2,1)S(1)}, u32[]{:S(2)}, u32[]{:S(2)}) collective-permute-start(bf16[128,576]{0,1:T(8,128)(2,1)} %param.5), channel_id=1, source_target_pairs={{0,56},{8,64},{16,72},{24,80},{32,88},{40,96},{48,104},{56,112},{6... | collective-permute-start | bytes 442376 | tf_op jit(solution)/shard_map/ppermute | solution.py:15
  22.2 51.3 %collective-permute-start.2 = (bf16[128,576]{0,1:T(8,128)(2,1)}, bf16[128,576]{0,1:T(8,128)(2,1)S(1)}, u32[]{:S(2)}, u32[]{:S(2)}) collective-permute-start(bf16[128,576]{0,1:T(8,128)(2,1)} %param.5), channel_id=1, source_target_pairs={{0,48},{8,56},{16,64},{24,72},{32,80},{40,88},{48,96},{56,104},{64... | collective-permute-start | bytes 442376 | tf_op jit(solution)/shard_map/ppermute | solution.py:15
  26.5 64.8 %collective-permute-start.3 = (bf16[128,576]{0,1:T(8,128)(2,1)}, bf16[128,576]{0,1:T(8,128)(2,1)S(1)}, u32[]{:S(2)}, u32[]{:S(2)}) collective-permute-start(bf16[128,576]{0,1:T(8,128)(2,1)} %param.5), channel_id=1, source_target_pairs={{0,40},{8,48},{16,56},{24,64},{32,72},{40,80},{48,88},{56,96},{64,... | collective-permute-start | bytes 442376 | tf_op jit(solution)/shard_map/ppermute | solution.py:15
  35.2 56.9 %collective-permute-start.4 = (bf16[128,576]{0,1:T(8,128)(2,1)}, bf16[128,576]{0,1:T(8,128)(2,1)S(1)}, u32[]{:S(2)}, u32[]{:S(2)}) collective-permute-start(bf16[128,576]{0,1:T(8,128)(2,1)} %param.5), channel_id=1, source_target_pairs={{0,32},{8,40},{16,48},{24,56},{32,64},{40,72},{48,80},{56,88},{64,... | collective-permute-start | bytes 442376 | tf_op jit(solution)/shard_map/ppermute | solution.py:15
  43.8 64.0 %collective-permute-start.5 = (bf16[128,576]{0,1:T(8,128)(2,1)S(1)}, bf16[128,576]{0,1:T(8,128)(2,1)S(1)}, u32[]{:S(2)}, u32[]{:S(2)}) collective-permute-start(bf16[128,576]{0,1:T(8,128)(2,1)S(1)} %copy-done.1), channel_id=1, source_target_pairs={{0,24},{8,32},{16,40},{24,48},{32,56},{40,64},{48,72},{56,80},{64,... | collective-permute-start | bytes 442376 | tf_op jit(solution)/shard_map/ppermute | solution.py:15
  64.6 50.1 %collective-permute-start.6 = (bf16[128,576]{0,1:T(8,128)(2,1)S(1)}, bf16[128,576]{0,1:T(8,128)(2,1)S(1)}, u32[]{:S(2)}, u32[]{:S(2)}) collective-permute-start(bf16[128,576]{0,1:T(8,128)(2,1)S(1)} %copy-done.1), channel_id=1, source_target_pairs={{0,16},{8,24},{16,32},{24,40},{32,48},{40,56},{48,64},{56,72},{64,... | collective-permute-start | bytes 442376 | tf_op jit(solution)/shard_map/ppermute | solution.py:15
  73.5 44.2 %collective-permute-start.7 = (bf16[128,576]{0,1:T(8,128)(2,1)S(1)}, bf16[128,576]{0,1:T(8,128)(2,1)S(1)}, u32[]{:S(2)}, u32[]{:S(2)}) collective-permute-start(bf16[128,576]{0,1:T(8,128)(2,1)S(1)} %copy-done.1), channel_id=1, source_target_pairs={{0,8},{8,16},{16,24},{24,32},{32,40},{40,48},{48,56},{56,64},{64,7... | collective-permute-start | bytes 442376 | tf_op jit(solution)/shard_map/ppermute | solution.py:15
  125.8 4.4 %copy-start.2 = (f32[8,128,1152]{1,2,0:T(8,128)S(1)}, f32[8,128,1152]{1,2,0:T(8,128)}, u32[]{:S(2)}) copy-start(f32[8,128,1152]{1,2,0:T(8,128)} %get-tuple-element.11) | copy-start | bytes 14155780
  136.9 38.7 %collective-permute-start.15 = (f32[128,576]{0,1:T(8,128)S(1)}, f32[128,576]{0,1:T(8,128)S(1)}, u32[]{:S(2)}, u32[]{:S(2)}) collective-permute-start(f32[128,576]{0,1:T(8,128)S(1)} %get-tuple-element.3), channel_id=1, source_target_pairs={{64,0},{72,8},{80,16},{88,24},{96,32},{104,40},{112,48},{120,56},{... | collective-permute-start | bytes 884744 | tf_op jit(solution)/shard_map/ppermute | solution.py:15
  146.1 60.5 %collective-permute-start.14 = (f32[128,576]{0,1:T(8,128)S(1)}, f32[128,576]{0,1:T(8,128)S(1)}, u32[]{:S(2)}, u32[]{:S(2)}) collective-permute-start(f32[128,576]{0,1:T(8,128)S(1)} %get-tuple-element.4), channel_id=1, source_target_pairs={{56,0},{64,8},{72,16},{80,24},{88,32},{96,40},{104,48},{112,56},{1... | collective-permute-start | bytes 884744 | tf_op jit(solution)/shard_map/ppermute | solution.py:15
  151.6 103.3 %collective-permute-start.13 = (f32[128,576]{0,1:T(8,128)S(1)}, f32[128,576]{0,1:T(8,128)S(1)}, u32[]{:S(2)}, u32[]{:S(2)}) collective-permute-start(f32[128,576]{0,1:T(8,128)S(1)} %get-tuple-element.5), channel_id=1, source_target_pairs={{48,0},{56,8},{64,16},{72,24},{80,32},{88,40},{96,48},{104,56},{11... | collective-permute-start | bytes 884744 | tf_op jit(solution)/shard_map/ppermute | solution.py:15
  155.7 130.2 %collective-permute-start.12 = (f32[128,576]{0,1:T(8,128)S(1)}, f32[128,576]{0,1:T(8,128)S(1)}, u32[]{:S(2)}, u32[]{:S(2)}) collective-permute-start(f32[128,576]{0,1:T(8,128)S(1)} %get-tuple-element.6), channel_id=1, source_target_pairs={{40,0},{48,8},{56,16},{64,24},{72,32},{80,40},{88,48},{96,56},{104... | collective-permute-start | bytes 884744 | tf_op jit(solution)/shard_map/ppermute | solution.py:15
  164.1 146.9 %collective-permute-start.11 = (f32[128,576]{0,1:T(8,128)S(1)}, f32[128,576]{0,1:T(8,128)S(1)}, u32[]{:S(2)}, u32[]{:S(2)}) collective-permute-start(f32[128,576]{0,1:T(8,128)S(1)} %get-tuple-element.7), channel_id=1, source_target_pairs={{32,0},{40,8},{48,16},{56,24},{64,32},{72,40},{80,48},{88,56},{96,... | collective-permute-start | bytes 884744 | tf_op jit(solution)/shard_map/ppermute | solution.py:15
  175.6 153.1 %collective-permute-start.10 = (f32[128,576]{0,1:T(8,128)S(1)}, f32[128,576]{0,1:T(8,128)S(1)}, u32[]{:S(2)}, u32[]{:S(2)}) collective-permute-start(f32[128,576]{0,1:T(8,128)S(1)} %get-tuple-element.8), channel_id=1, source_target_pairs={{24,0},{32,8},{40,16},{48,24},{56,32},{64,40},{72,48},{80,56},{88,... | collective-permute-start | bytes 884744 | tf_op jit(solution)/shard_map/ppermute | solution.py:15
  206.6 134.5 %collective-permute-start.9 = (f32[128,576]{0,1:T(8,128)S(1)}, f32[128,576]{0,1:T(8,128)S(1)}, u32[]{:S(2)}, u32[]{:S(2)}) collective-permute-start(f32[128,576]{0,1:T(8,128)S(1)} %get-tuple-element.9), channel_id=1, source_target_pairs={{16,0},{24,8},{32,16},{40,24},{48,32},{56,40},{64,48},{72,56},{80,... | collective-permute-start | bytes 884744 | tf_op jit(solution)/shard_map/ppermute | solution.py:15
  254.9 92.6 %collective-permute-start.8 = (f32[128,576]{0,1:T(8,128)S(1)}, f32[128,576]{0,1:T(8,128)S(1)}, u32[]{:S(2)}, u32[]{:S(2)}) collective-permute-start(f32[128,576]{0,1:T(8,128)S(1)} %get-tuple-element.2), channel_id=1, source_target_pairs={{8,0},{16,8},{24,16},{32,24},{40,32},{48,40},{56,48},{64,56},{72,6... | collective-permute-start | bytes 884744 | tf_op jit(solution)/shard_map/ppermute | solution.py:15
where the time goes:
time: 378 us; the launch traced here: 377 us
  waiting for transfers between devices  203 us (54%)
  starting transfers between devices  112 us (30%)
  blocking collectives  29.4 us (8%)
  matrix products  21.6 us (6%)
  local copies, waits for them, and re-layouts  9.14 us (2%)
    ppermute x16, waiting for transfers between devices, passed_along(): lax.ppermute(value, axis, [(source, source + steps) for source in range(l...  203 us
    ppermute x16, starting transfers between devices, passed_along(): lax.ppermute(value, axis, [(source, source + steps) for source in range(l...  112 us
    psum x1, blocking collectives, on_device(): owned = lax.psum(return_owned(grad_keys, tok_rows), 'head')  29.4 us
  transfers between devices with their start and end apart: 16, of which 13 were waited for; matrix products, arithmetic and copies ran while one was open for 3% of the time, Pallas kernels for 0%

commit v1 on v0

--- a/solution.py
+++ b/solution.py
@@ -70,7 +70,7 @@
     key_pos = start - SPAN * tok_rows + jnp.arange(window, dtype=jnp.int32)
     visible = (key_ids[None, :] == query_ids[:, None]) & (key_pos[None, :] <= query_pos[:, None])
     grad_query, grad_keys = attend_backward(queries, grad_out, key_rows, visible)
-    owned = lax.psum(return_owned(grad_keys, tok_rows), "head")
+    owned = jnp.sum(lax.all_gather(return_owned(grad_keys, tok_rows), "head"), axis=0)
     return (grad_query, owned.astype(jnp.bfloat16))
 
 

time: 378 us -> 402 us (1.063)
  the two profiles are of different devices: /device:TPU:16 before, /device:TPU:1 now
where the time goes in v1:
time: 402 us; the launch traced here: 401 us
  waiting for transfers between devices  285 us (71%)
  starting transfers between devices  64.4 us (16%)
  matrix products  21.6 us (5%)
  between operations  14.3 us (4%)
  local copies, waits for them, and re-layouts  11.4 us (3%)
    ppermute x16, waiting for transfers between devices, passed_along(): lax.ppermute(value, axis, [(source, source + steps) for source in range(l...  166 us
    all_gather x1, waiting for transfers between devices, on_device(): lax.all_gather(return_owned(grad_keys, tok_rows), 'head')  119 us
    ppermute x16, starting transfers between devices, passed_along(): lax.ppermute(value, axis, [(source, source + steps) for source in range(l...  64.3 us
    unnamed x20, local copies, waits for them, and re-layouts  9.73 us
  transfers between devices with their start and end apart: 17, of which 13 were waited for; matrix products, arithmetic and copies ran while one was open for 3% of the time, Pallas kernels for 0%

profile of v1, /device:TPU:1, one launch (start us, length us, event | category | flops | bytes accessed | tf_op | source)
XLA Modules:
  0.0 400.8 jit_solution(2641458598447823965)
XLA Ops:
  7.2 16.4 %collective-permute-start = (bf16[128,576]{0,1:T(8,128)(2,1)}, bf16[128,576]{0,1:T(8,128)(2,1)S(1)}, u32[]{:S(2)}, u32[]{:S(2)}) collective-permute-start(bf16[128,576]{0,1:T(8,128)(2,1)} %param.5), channel_id=1, source_target_pairs={{0,64},{8,72},{16,80},{24,88},{32,96},{40,104},{48,112},{56,120},{... | collective-permute-start | bytes 442376 | tf_op jit(solution)/shard_map/ppermute | solution.py:15
  23.6 5.4 %collective-permute-start.1 = (bf16[128,576]{0,1:T(8,128)(2,1)}, bf16[128,576]{0,1:T(8,128)(2,1)S(1)}, u32[]{:S(2)}, u32[]{:S(2)}) collective-permute-start(bf16[128,576]{0,1:T(8,128)(2,1)} %param.5), channel_id=1, source_target_pairs={{0,56},{8,64},{16,72},{24,80},{32,88},{40,96},{48,104},{56,112},{6... | collective-permute-start | bytes 442376 | tf_op jit(solution)/shard_map/ppermute | solution.py:15
  29.0 4.4 %collective-permute-start.2 = (bf16[128,576]{0,1:T(8,128)(2,1)}, bf16[128,576]{0,1:T(8,128)(2,1)S(1)}, u32[]{:S(2)}, u32[]{:S(2)}) collective-permute-start(bf16[128,576]{0,1:T(8,128)(2,1)} %param.5), channel_id=1, source_target_pairs={{0,48},{8,56},{16,64},{24,72},{32,80},{40,88},{48,96},{56,104},{64... | collective-permute-start | bytes 442376 | tf_op jit(solution)/shard_map/ppermute | solution.py:15
  33.4 8.4 %collective-permute-start.3 = (bf16[128,576]{0,1:T(8,128)(2,1)}, bf16[128,576]{0,1:T(8,128)(2,1)S(1)}, u32[]{:S(2)}, u32[]{:S(2)}) collective-permute-start(bf16[128,576]{0,1:T(8,128)(2,1)} %param.5), channel_id=1, source_target_pairs={{0,40},{8,48},{16,56},{24,64},{32,72},{40,80},{48,88},{56,96},{64,... | collective-permute-start | bytes 442376 | tf_op jit(solution)/shard_map/ppermute | solution.py:15
  41.8 4.0 %collective-permute-start.4 = (bf16[128,576]{0,1:T(8,128)(2,1)}, bf16[128,576]{0,1:T(8,128)(2,1)S(1)}, u32[]{:S(2)}, u32[]{:S(2)}) collective-permute-start(bf16[128,576]{0,1:T(8,128)(2,1)} %param.5), channel_id=1, source_target_pairs={{0,32},{8,40},{16,48},{24,56},{32,64},{40,72},{48,80},{56,88},{64,... | collective-permute-start | bytes 442376 | tf_op jit(solution)/shard_map/ppermute | solution.py:15
  48.1 1.9 copy.8
  52.1 2.7 collective-permute-done.1
  56.8 12.2 %collective-permute-done.2 = bf16[128,576]{0,1:T(8,128)(2,1)S(1)} collective-permute-done((bf16[128,576]{0,1:T(8,128)(2,1)}, bf16[128,576]{0,1:T(8,128)(2,1)S(1)}, u32[]{:S(2)}, u32[]{:S(2)}) %collective-permute-start.2) | collective-permute-done | bytes 147488 | tf_op jit(solution)/shard_map/ppermute | solution.py:15
  69.0 12.6 %collective-permute-start.7 = (bf16[128,576]{0,1:T(8,128)(2,1)S(1)}, bf16[128,576]{0,1:T(8,128)(2,1)S(1)}, u32[]{:S(2)}, u32[]{:S(2)}) collective-permute-start(bf16[128,576]{0,1:T(8,128)(2,1)S(1)} %copy-done.1), channel_id=1, source_target_pairs={{0,8},{8,16},{16,24},{24,32},{32,40},{40,48},{48,56},{56,64},{64,7... | collective-permute-start | bytes 442376 | tf_op jit(solution)/shard_map/ppermute | solution.py:15
  82.3 9.9 %collective-permute-done.3 = bf16[128,576]{0,1:T(8,128)(2,1)S(1)} collective-permute-done((bf16[128,576]{0,1:T(8,128)(2,1)}, bf16[128,576]{0,1:T(8,128)(2,1)S(1)}, u32[]{:S(2)}, u32[]{:S(2)}) %collective-permute-start.3) | collective-permute-done | bytes 147488 | tf_op jit(solution)/shard_map/ppermute | solution.py:15
  93.0 4.9 %collective-permute-done.4 = bf16[128,576]{0,1:T(8,128)(2,1)S(1)} collective-permute-done((bf16[128,576]{0,1:T(8,128)(2,1)}, bf16[128,576]{0,1:T(8,128)(2,1)S(1)}, u32[]{:S(2)}, u32[]{:S(2)}) %collective-permute-start.4) | collective-permute-done | bytes 147488 | tf_op jit(solution)/shard_map/ppermute | solution.py:15
  98.6 16.0 %collective-permute-done.5 = bf16[128,576]{0,1:T(8,128)(2,1)S(1)} collective-permute-done((bf16[128,576]{0,1:T(8,128)(2,1)S(1)}, bf16[128,576]{0,1:T(8,128)(2,1)S(1)}, u32[]{:S(2)}, u32[]{:S(2)}) %collective-permute-start.5) | collective-permute-done | bytes 147488 | tf_op jit(solution)/shard_map/ppermute | solution.py:15
  115.2 4.7 %collective-permute-done.6 = bf16[128,576]{0,1:T(8,128)(2,1)S(1)} collective-permute-done((bf16[128,576]{0,1:T(8,128)(2,1)S(1)}, bf16[128,576]{0,1:T(8,128)(2,1)S(1)}, u32[]{:S(2)}, u32[]{:S(2)}) %collective-permute-start.6) | collective-permute-done | bytes 147488 | tf_op jit(solution)/shard_map/ppermute | solution.py:15
  120.6 4.0 %collective-permute-done.7 = bf16[128,576]{0,1:T(8,128)(2,1)S(1)} collective-permute-done((bf16[128,576]{0,1:T(8,128)(2,1)S(1)}, bf16[128,576]{0,1:T(8,128)(2,1)S(1)}, u32[]{:S(2)}, u32[]{:S(2)}) %collective-permute-start.7) | collective-permute-done | bytes 147488 | tf_op jit(solution)/shard_map/ppermute | solution.py:15
  126.0 6.8 %fusion.25 = (f32[8,128]{1,0:T(8,128)S(1)}, f32[8,128,1152]{1,2,0:T(8,128)}) fusion(pred[128,1152]{0,1:T(8,128)(4,1)S(1)} %compare_and_fusion, bf16[128,8,576]{0,2,1:T(8,128)(2,1)S(1)} %copy-done, bf16[1152,576]{0,1:T(8,128)(2,1)} %constant_dynamic-update-slice_fusion), kind=kOutput, calls=%fused_computation.48 | convolution fusion | flops 1364853888 | bytes 7376896 | tf_op jit(solution)/shard_map/sub | solution.py:26
  132.8 4.4 %fusion.9 = f32[128,8]{0,1:T(8,128)S(1)} fusion(bf16[128,8,512]{0,2,1:T(8,128)(2,1)S(1)} %copy.8, bf16[1152,576]{0,1:T(8,128)(2,1)} %constant_dynamic-update-slice_fusion, f32[8,128,1152]{1,2,0:T(8,128)} %get-tuple-element.11, f32[8,128]{1,0:T(8,128)S(1)} %get-tuple-element.10), kind=kOutput, calls=%fused_computation.18 | convolution fusion | flops 1211890688 | bytes 6955008 | tf_op jit(solution)/shard_map/htk,kc->thc/dot_general | solution.py:29
  138.8 3.1 fusion.4
  150.5 12.3 %collective-permute-done.15 = f32[128,576]{0,1:T(8,128)S(1)} collective-permute-done((f32[128,576]{0,1:T(8,128)S(1)}, f32[128,576]{0,1:T(8,128)S(1)}, u32[]{:S(2)}, u32[]{:S(2)}) %collective-permute-start.15) | collective-permute-done | bytes 294944 | tf_op jit(solution)/shard_map/ppermute | solution.py:15
  167.2 76.9 %collective-permute-done.13 = f32[128,576]{0,1:T(8,128)S(1)} collective-permute-done((f32[128,576]{0,1:T(8,128)S(1)}, f32[128,576]{0,1:T(8,128)S(1)}, u32[]{:S(2)}, u32[]{:S(2)}) %collective-permute-start.13) | collective-permute-done | bytes 294944 | tf_op jit(solution)/shard_map/ppermute | solution.py:15
  245.6 11.9 %collective-permute-done.10 = f32[128,576]{0,1:T(8,128)S(1)} collective-permute-done((f32[128,576]{0,1:T(8,128)S(1)}, f32[128,576]{0,1:T(8,128)S(1)}, u32[]{:S(2)}, u32[]{:S(2)}) %collective-permute-start.10) | collective-permute-done | bytes 294944 | tf_op jit(solution)/shard_map/ppermute | solution.py:15
  257.5 9.0 %collective-permute-done.9 = f32[128,576]{0,1:T(8,128)S(1)} collective-permute-done((f32[128,576]{0,1:T(8,128)S(1)}, f32[128,576]{0,1:T(8,128)S(1)}, u32[]{:S(2)}, u32[]{:S(2)}) %collective-permute-start.9) | collective-permute-done | bytes 294944 | tf_op jit(solution)/shard_map/ppermute | solution.py:15
  267.5 4.0 %fusion.11 = bf16[128,8,576]{0,2,1:T(8,128)(2,1)} fusion(bf16[8,128,1152]{1,2,0:T(8,128)(2,1)S(1)} %copy-done.3, bf16[1152,576]{0,1:T(8,128)(2,1)} %constant_dynamic-update-slice_fusion), kind=kOutput, calls=%fused_computation.21 | convolution fusion | flops 1359544320 | bytes 4866048 | tf_op jit(solution)/shard_map/htk,kc->thc/dot_general | solution.py:37
  271.5 119.0 %all-gather.3.cloned.1.call-done = f32[1024,576]{0,1:T(8,128)} async-done(((f32[128,576]{0,1:T(8,128)}), f32[1024,576]{0,1:T(8,128)}) %all-gather.3.cloned.1.call-update) | async-done | bytes 2359312 | tf_op jit(solution)/shard_map/all_gather | solution.py:73
  390.5 2.2 copy.20
  (45 shorter events, 29.5 us)
Async XLA Ops:
  7.2 118.9 %copy-start = (bf16[128,8,576]{0,2,1:T(8,128)(2,1)S(1)}, bf16[128,8,576]{0,2,1:T(8,128)(2,1)}, u32[]{:S(2)}) copy-start(bf16[128,8,576]{0,2,1:T(8,128)(2,1)} %param.4) | copy-start | bytes 3538948
  7.2 42.9 %copy-start.1 = (bf16[128,576]{0,1:T(8,128)(2,1)S(1)}, bf16[128,576]{0,1:T(8,128)(2,1)}, u32[]{:S(2)}) copy-start(bf16[128,576]{0,1:T(8,128)(2,1)} %param.5) | copy-start | bytes 442372
  7.2 383.3 %all-gather.3.cloned.1.call-start = ((), (), s32[]{:S(2)}) async-start(), calls=%async_computation | async-start | bytes 2654208 | tf_op jit(solution)/shard_map/all_gather | solution.py:73
  7.2 42.9 %collective-permute-start = (bf16[128,576]{0,1:T(8,128)(2,1)}, bf16[128,576]{0,1:T(8,128)(2,1)S(1)}, u32[]{:S(2)}, u32[]{:S(2)}) collective-permute-start(bf16[128,576]{0,1:T(8,128)(2,1)} %param.5), channel_id=1, source_target_pairs={{0,64},{8,72},{16,80},{24,88},{32,96},{40,104},{48,112},{56,120},{... | collective-permute-start | bytes 442376 | tf_op jit(solution)/shard_map/ppermute | solution.py:15
  23.6 31.1 %collective-permute-start.1 = (bf16[128,576]{0,1:T(8,128)(2,1)}, bf16[128,576]{0,1:T(8,128)(2,1)S(1)}, u32[]{:S(2)}, u32[]{:S(2)}) collective-permute-start(bf16[128,576]{0,1:T(8,128)(2,1)} %param.5), channel_id=1, source_target_pairs={{0,56},{8,64},{16,72},{24,80},{32,88},{40,96},{48,104},{56,112},{6... | collective-permute-start | bytes 442376 | tf_op jit(solution)/shard_map/ppermute | solution.py:15
  29.0 40.0 %collective-permute-start.2 = (bf16[128,576]{0,1:T(8,128)(2,1)}, bf16[128,576]{0,1:T(8,128)(2,1)S(1)}, u32[]{:S(2)}, u32[]{:S(2)}) collective-permute-start(bf16[128,576]{0,1:T(8,128)(2,1)} %param.5), channel_id=1, source_target_pairs={{0,48},{8,56},{16,64},{24,72},{32,80},{40,88},{48,96},{56,104},{64... | collective-permute-start | bytes 442376 | tf_op jit(solution)/shard_map/ppermute | solution.py:15
  33.4 58.8 %collective-permute-start.3 = (bf16[128,576]{0,1:T(8,128)(2,1)}, bf16[128,576]{0,1:T(8,128)(2,1)S(1)}, u32[]{:S(2)}, u32[]{:S(2)}) collective-permute-start(bf16[128,576]{0,1:T(8,128)(2,1)} %param.5), channel_id=1, source_target_pairs={{0,40},{8,48},{16,56},{24,64},{32,72},{40,80},{48,88},{56,96},{64,... | collective-permute-start | bytes 442376 | tf_op jit(solution)/shard_map/ppermute | solution.py:15
  41.8 56.1 %collective-permute-start.4 = (bf16[128,576]{0,1:T(8,128)(2,1)}, bf16[128,576]{0,1:T(8,128)(2,1)S(1)}, u32[]{:S(2)}, u32[]{:S(2)}) collective-permute-start(bf16[128,576]{0,1:T(8,128)(2,1)} %param.5), channel_id=1, source_target_pairs={{0,32},{8,40},{16,48},{24,56},{32,64},{40,72},{48,80},{56,88},{64,... | collective-permute-start | bytes 442376 | tf_op jit(solution)/shard_map/ppermute | solution.py:15
  50.1 64.4 %collective-permute-start.5 = (bf16[128,576]{0,1:T(8,128)(2,1)S(1)}, bf16[128,576]{0,1:T(8,128)(2,1)S(1)}, u32[]{:S(2)}, u32[]{:S(2)}) collective-permute-start(bf16[128,576]{0,1:T(8,128)(2,1)S(1)} %copy-done.1), channel_id=1, source_target_pairs={{0,24},{8,32},{16,40},{24,48},{32,56},{40,64},{48,72},{56,80},{64,... | collective-permute-start | bytes 442376 | tf_op jit(solution)/shard_map/ppermute | solution.py:15
  54.8 65.1 %collective-permute-start.6 = (bf16[128,576]{0,1:T(8,128)(2,1)S(1)}, bf16[128,576]{0,1:T(8,128)(2,1)S(1)}, u32[]{:S(2)}, u32[]{:S(2)}) collective-permute-start(bf16[128,576]{0,1:T(8,128)(2,1)S(1)} %copy-done.1), channel_id=1, source_target_pairs={{0,16},{8,24},{16,32},{24,40},{32,48},{40,56},{48,64},{56,72},{64,... | collective-permute-start | bytes 442376 | tf_op jit(solution)/shard_map/ppermute | solution.py:15
  69.0 55.6 %collective-permute-start.7 = (bf16[128,576]{0,1:T(8,128)(2,1)S(1)}, bf16[128,576]{0,1:T(8,128)(2,1)S(1)}, u32[]{:S(2)}, u32[]{:S(2)}) collective-permute-start(bf16[128,576]{0,1:T(8,128)(2,1)S(1)} %copy-done.1), channel_id=1, source_target_pairs={{0,8},{8,16},{16,24},{24,32},{32,40},{40,48},{48,56},{56,64},{64,7... | collective-permute-start | bytes 442376 | tf_op jit(solution)/shard_map/ppermute | solution.py:15
  132.8 4.4 %copy-start.4 = (f32[8,128,1152]{1,2,0:T(8,128)S(1)}, f32[8,128,1152]{1,2,0:T(8,128)}, u32[]{:S(2)}) copy-start(f32[8,128,1152]{1,2,0:T(8,128)} %get-tuple-element.11) | copy-start | bytes 14155780
  141.9 1.8 copy-start.2
  143.8 123.6 %copy-start.3 = (bf16[8,128,1152]{1,2,0:T(8,128)(2,1)S(1)}, bf16[8,128,1152]{1,2,0:T(8,128)(2,1)}, u32[]{:S(2)}) copy-start(bf16[8,128,1152]{1,2,0:T(8,128)(2,1)} %copy-done.2) | copy-start | bytes 7077892
  143.9 18.9 %collective-permute-start.15 = (f32[128,576]{0,1:T(8,128)S(1)}, f32[128,576]{0,1:T(8,128)S(1)}, u32[]{:S(2)}, u32[]{:S(2)}) collective-permute-start(f32[128,576]{0,1:T(8,128)S(1)} %get-tuple-element.3), channel_id=1, source_target_pairs={{64,0},{72,8},{80,16},{88,24},{96,32},{104,40},{112,48},{120,56},{... | collective-permute-start | bytes 884744 | tf_op jit(solution)/shard_map/ppermute | solution.py:15
  145.3 20.6 %collective-permute-start.14 = (f32[128,576]{0,1:T(8,128)S(1)}, f32[128,576]{0,1:T(8,128)S(1)}, u32[]{:S(2)}, u32[]{:S(2)}) collective-permute-start(f32[128,576]{0,1:T(8,128)S(1)} %get-tuple-element.4), channel_id=1, source_target_pairs={{56,0},{64,8},{72,16},{80,24},{88,32},{96,40},{104,48},{112,56},{1... | collective-permute-start | bytes 884744 | tf_op jit(solution)/shard_map/ppermute | solution.py:15
  146.6 97.6 %collective-permute-start.13 = (f32[128,576]{0,1:T(8,128)S(1)}, f32[128,576]{0,1:T(8,128)S(1)}, u32[]{:S(2)}, u32[]{:S(2)}) collective-permute-start(f32[128,576]{0,1:T(8,128)S(1)} %get-tuple-element.5), channel_id=1, source_target_pairs={{48,0},{56,8},{64,16},{72,24},{80,32},{88,40},{96,48},{104,56},{11... | collective-permute-start | bytes 884744 | tf_op jit(solution)/shard_map/ppermute | solution.py:15
  147.9 97.7 %collective-permute-start.12 = (f32[128,576]{0,1:T(8,128)S(1)}, f32[128,576]{0,1:T(8,128)S(1)}, u32[]{:S(2)}, u32[]{:S(2)}) collective-permute-start(f32[128,576]{0,1:T(8,128)S(1)} %get-tuple-element.6), channel_id=1, source_target_pairs={{40,0},{48,8},{56,16},{64,24},{72,32},{80,40},{88,48},{96,56},{104... | collective-permute-start | bytes 884744 | tf_op jit(solution)/shard_map/ppermute | solution.py:15
  149.2 96.4 %collective-permute-start.11 = (f32[128,576]{0,1:T(8,128)S(1)}, f32[128,576]{0,1:T(8,128)S(1)}, u32[]{:S(2)}, u32[]{:S(2)}) collective-permute-start(f32[128,576]{0,1:T(8,128)S(1)} %get-tuple-element.7), channel_id=1, source_target_pairs={{32,0},{40,8},{48,16},{56,24},{64,32},{72,40},{80,48},{88,56},{96,... | collective-permute-start | bytes 884744 | tf_op jit(solution)/shard_map/ppermute | solution.py:15
  162.7 94.8 %collective-permute-start.10 = (f32[128,576]{0,1:T(8,128)S(1)}, f32[128,576]{0,1:T(8,128)S(1)}, u32[]{:S(2)}, u32[]{:S(2)}) collective-permute-start(f32[128,576]{0,1:T(8,128)S(1)} %get-tuple-element.8), channel_id=1, source_target_pairs={{24,0},{32,8},{40,16},{48,24},{56,32},{64,40},{72,48},{80,56},{88,... | collective-permute-start | bytes 884744 | tf_op jit(solution)/shard_map/ppermute | solution.py:15
  165.9 100.6 %collective-permute-start.9 = (f32[128,576]{0,1:T(8,128)S(1)}, f32[128,576]{0,1:T(8,128)S(1)}, u32[]{:S(2)}, u32[]{:S(2)}) collective-permute-start(f32[128,576]{0,1:T(8,128)S(1)} %get-tuple-element.9), channel_id=1, source_target_pairs={{16,0},{24,8},{32,16},{40,24},{48,32},{56,40},{64,48},{72,56},{80,... | collective-permute-start | bytes 884744 | tf_op jit(solution)/shard_map/ppermute | solution.py:15
  244.1 22.4 %collective-permute-start.8 = (f32[128,576]{0,1:T(8,128)S(1)}, f32[128,576]{0,1:T(8,128)S(1)}, u32[]{:S(2)}, u32[]{:S(2)}) collective-permute-start(f32[128,576]{0,1:T(8,128)S(1)} %get-tuple-element.2), channel_id=1, source_target_pairs={{8,0},{16,8},{24,16},{32,24},{40,32},{48,40},{56,48},{64,56},{72,6... | collective-permute-start | bytes 884744 | tf_op jit(solution)/shard_map/ppermute | solution.py:15
Sparse Core Ops, SparseCore 0:
  267.6 122.8 all-gather.2
